TPU v7x, 128 devices: a whole 4x4x4 slice. The times are simulated.
128 devices in a mesh: band: 4 (over z_hi, core), dom: 32 (over y, z_lo, x).
Axes of the slice: x: 4, y: 4, z: 4 (z_hi: 2, z_lo: 2; z = z_hi * 2 + z_lo), core: 2. Of those that a mesh axis runs over, the one named last changes fastest.
Arguments:
- orbitals: bfloat16 [512, 128, 32, 256], P('band', 'dom'), may hold values from -0.1875 to 0.1875
- potential: float32 [128, 32, 256], P('dom'), may hold values from 0.5 to 2.5
- projectors: bfloat16 [128, 128, 32, 256], P(None, 'dom'), may hold values from -0.1875 to 0.1875
- coupling: float32 [128], replicated, may hold values from -1 to 1
- pattern: int32 [8, 2], P('band'), may hold values 0 or 1
Outputs:
- correlation_next: float32 [512, 128], P(('band', 'dom'))
- hamiltonian_next: float32 [512, 128], P(('band', 'dom'))
All inputs are finite; a program needn't handle non-finite values. No bound on the sum of `pattern` on one device may be relied on, other than what follows from the above.
Results may differ from a plain program's by a relative error of at most 0.0033.
The roundings to bfloat16 on the way count: a program that leaves them out, or rounds other values in their place, can miss the bound.
Values may be sent and summed in bfloat16 or wider, within the bound.
A program may use at most 384 MiB of HBM per device.

v0:
```python
import jax
import jax.numpy as jnp
from jax import lax
from jax.sharding import PartitionSpec as P

BLOCK = 64


C0 = -2.5
C1 = 4.0 / 3.0
C2 = -1.0 / 12.0


def extended(cells, sides, width):
    for axis, dim in sides:
        count = lax.axis_size(axis)
        head = lax.slice_in_dim(cells, 0, width, axis=dim)
        tail = lax.slice_in_dim(cells, cells.shape[dim] - width, cells.shape[dim], axis=dim)
        cells = jnp.concatenate(
            [
                lax.ppermute(tail, axis, [(i, (i + 1) % count) for i in range(count)]),
                cells,
                lax.ppermute(head, axis, [((i + 1) % count, i) for i in range(count)]),
            ],
            axis=dim,
        )
    return cells


def shifted(value, axis, steps):
    count = lax.axis_size(axis)
    pairs = [(source, (source + steps) % count) for source in range(count)]
    return lax.ppermute(value, axis, pairs)


def local_apply(padded, potential):
    center = padded[:, 2:-2].astype(jnp.float32)
    near = padded[:, 3:-1].astype(jnp.float32) + padded[:, 1:-3].astype(jnp.float32)
    far = padded[:, 4:].astype(jnp.float32) + padded[:, :-4].astype(jnp.float32)
    for axis in (2, 3):
        near = near + jnp.roll(center, 1, axis) + jnp.roll(center, -1, axis)
        far = far + jnp.roll(center, 2, axis) + jnp.roll(center, -2, axis)
    kinetic = -0.5 * (3.0 * C0 * center + C1 * near + C2 * far)
    return kinetic + potential[None] * center


def contract_cells(left, right):
    return lax.dot_general(
        left, right, (((1,), (1,)), ((), ())), preferred_element_type=jnp.float32
    )


def pair_products(left, right, right_images):
    return jnp.stack([contract_cells(left, right), contract_cells(left, right_images)])


def domain_rows(terms):
    return lax.psum_scatter(terms, "dom", scatter_dimension=1, tiled=True)


def on_device(orbitals, potential, projectors, coupling, pattern):
    count, width, extent_y, extent_z = orbitals.shape
    cells = width * extent_y * extent_z
    padded = extended(orbitals, (("dom", 1),), 2)
    blocks = padded.reshape(count // BLOCK, BLOCK, width + 4, extent_y, extent_z)
    local_part = lax.map(lambda blk: local_apply(blk, potential), blocks).reshape(count, cells)
    flat = orbitals.reshape(count, cells)
    proj_flat = projectors.reshape(projectors.shape[0], cells)
    partial_coef = contract_cells(proj_flat, flat)
    coef = lax.psum(partial_coef, "dom")
    weighted = (coupling[:, None] * coef).astype(jnp.bfloat16)
    nonlocal_part = lax.dot_general(
        weighted, proj_flat, (((0,), (0,)), ((), ())), preferred_element_type=jnp.float32
    )
    images = (local_part + nonlocal_part).astype(jnp.bfloat16)
    next_flat, next_images = shifted((flat, images), "band", -1)
    reduced = domain_rows(pair_products(flat, next_flat, next_images))
    mask_full = jnp.repeat(jnp.repeat(pattern.astype(jnp.float32), BLOCK, 0), BLOCK, 1)
    rows = count // lax.axis_size("dom")
    mine = lax.dynamic_slice_in_dim(mask_full, lax.axis_index("dom") * rows, rows, 0)
    masked = reduced * mine[None]
    return (masked[0], masked[1])


def solution(mesh):
    return jax.shard_map(
        on_device,
        mesh=mesh,
        in_specs=(
            P("band", "dom", None, None),
            P("dom", None, None),
            P(None, "dom", None, None),
            P(),
            P("band", None),
        ),
        out_specs=(P(("band", "dom"), None), P(("band", "dom"), None)),
        check_vma=False,
    )
```

profile of v0, /device:TPU:0, one launch (start us, length us, event | category | flops | bytes accessed | tf_op | source)
XLA Modules:
  0.0 722.2 jit_solution(14531756051343193218)
XLA Ops:
  7.2 0.0 all-reduce.4.cloned.1.call-start
  7.2 0.0 copy-start
  7.2 7.4 %fusion.32 = (bf16[128,2,32,256]{3,2,1,0:T(8,128)(2,1)}, bf16[128,2,32,256]{3,2,1,0:T(8,128)(2,1)}) fusion(bf16[128,4,32,256]{3,2,1,0:T(8,128)(2,1)} %param.7), kind=kLoop, calls=%fused_computation.42 | loop fusion | bytes 16777216 | tf_op jit(solution)/shard_map/slice | solution.py:18
  14.6 1.6 collective-permute-start.1
  16.2 5.1 collective-permute-start.2
  21.2 0.0 copy-done
  21.2 21.6 %fusion.18 = f32[128,128]{1,0:T(8,128)} fusion(bf16[128,4,32,256]{3,2,1,0:T(8,128)(2,1)S(1)} %copy-done, bf16[128,4,32,256]{3,2,1,0:T(8,128)(2,1)} %param.9), kind=kOutput, calls=%fused_computation.24 | convolution fusion | flops 1073741824 | bytes 16842752 | tf_op jit(solution)/shard_map/dot_general | solution.py:48
  42.8 0.0 all-reduce.4.cloned.1.call-update
  42.8 0.3 all-reduce.6.cloned.1.call-start
  43.1 12.3 %copy.20 = bf16[16,8,128,256]{3,1,2,0:T(8,128)(2,1)} copy(bf16[16,8,128,256]{3,2,1,0:T(8,128)(2,1)} %bitcast.48) | data formatting | bytes 16777216
  55.4 3.0 collective-permute-start
  58.4 12.4 %copy.21 = bf16[16,8,128,256]{3,1,2,0:T(8,128)(2,1)} copy(bf16[16,8,128,256]{3,2,1,0:T(8,128)(2,1)} %bitcast.50) | data formatting | bytes 16777216
  70.8 0.0 copy-start.1
  70.8 42.5 %collective-permute-done.1 = bf16[128,2,32,256]{3,2,1,0:T(8,128)(2,1)} collective-permute-done((bf16[128,2,32,256]{3,2,1,0:T(8,128)(2,1)}, bf16[128,2,32,256]{3,2,1,0:T(8,128)(2,1)}, u32[]{:S(2)}, u32[]{:S(2)}) %collective-permute-start.1) | collective-permute-done | bytes 4194336 | tf_op jit(solution)/shard_map/ppermute | solution.py:21
  113.3 0.0 collective-permute-done.2
  113.3 13.8 %pad_maximum_fusion = bf16[128,8,32,256]{3,2,1,0:T(8,128)(2,1)} fusion(bf16[128,2,32,256]{3,2,1,0:T(8,128)(2,1)} %collective-permute-done.2, bf16[128,4,32,256]{3,2,1,0:T(8,128)(2,1)} %param.7, bf16[128,2,32,256]{3,2,1,0:T(8,128)(2,1)} %collective-permute-done.1), kind=kLoop, calls=%fused_computation.20 | loop fusion | flops 16777216 | bytes 33554432 | tf_op jit(solution)/shard_map/concatenate | solution.py:19
  127.1 0.0 copy-done.1
  127.1 175.2 %while.10 = (s32[]{:T(128)}, f32[2,64,4,32,256]{4,3,2,1,0:T(8,128)}, bf16[2,64,8,32,256]{4,3,2,1,0:T(8,128)(2,1)}, f32[4,32,256]{2,1,0:T(8,128)S(1)}, s32[]{:T(128)}) while((s32[]{:T(128)}, f32[2,64,4,32,256]{4,3,2,1,0:T(8,128)}, bf16[2,64,8,32,256]{4,3,2,1,0:T(8,128)(2,1)}, f32[4,32,256]{2,1,0:T(8,128)S(1)}, s32[]{:T(128)}) %tuple.56), condition=%wide.region_1.2_spmd, body=%wide.region_0.1_spmd.sunk | while | flops 67108864 | bytes 274367008 | solution.py:66
  127.5 8.4 %dynamic-slice_bitcast_fusion.2 = bf16[64,8,32,256]{3,2,1,0:T(8,128)(2,1)} fusion(bf16[2,64,8,32,256]{4,3,2,1,0:T(8,128)(2,1)} %get-tuple-element.122, s32[]{:T(128)} %get-tuple-element.115), kind=kLoop, calls=%fused_computation.16.clone.1 | loop fusion | bytes 16777220 | tf_op jit(solution)/shard_map/while/body/jit(dynamic_index_in_dim)/squeeze | solution.py:66
  135.9 3.2 slice_convert_fusion.2
  139.2 7.2 %fusion.49 = (f32[64,4,32,255]{3,2,1,0:T(8,128)}, f32[64,4,32,255]{3,2,1,0:T(8,128)}) fusion(f32[64,4,32,256]{3,2,1,0:T(8,128)S(1)} %slice_convert_fusion.2), kind=kLoop, calls=%fused_computation.38.clone.1 | loop fusion | bytes 33423360 | tf_op jit(solution)/shard_map/while/body/eval_jaxpr/jit(_roll_static)/slice | solution.py:41
  146.4 6.9 fusion.51
  153.4 7.2 fusion.53
  160.5 6.9 fusion.47
  167.4 3.5 fusion.50
  170.9 4.8 fusion.54
  175.8 1.2 fusion.52
  177.0 1.1 fusion.48
  178.1 36.9 %fusion.55 = f32[2,64,4,32,256]{4,3,2,1,0:T(8,128)} fusion(f32[2,64,4,32,256]{4,3,2,1,0:T(8,128)} %get-tuple-element.116, s32[]{:T(128)} %get-tuple-element.115, f32[64,4,31,256]{3,2,1,0:T(8,128)} %get-tuple-element.94, f32[64,4,1,256]{3,2,1,0:T(1,128)} %get-tuple-element.95, f32[64,4,1,256]{3,2,1,0:T(1,128)S(1)} %get-tuple-element.96, ...), kind=kLoop, calls=%fused_computation.10.clone.1 | loop fusion | flops 65011712 | bytes 110789120 | tf_op jit(solution)/shard_map/while/body/jit(dynamic_update_index_in_dim)/dynamic_update_slice | solution.py:66
  215.0 8.4 %dynamic-slice_bitcast_fusion.2 = bf16[64,8,32,256]{3,2,1,0:T(8,128)(2,1)} fusion(bf16[2,64,8,32,256]{4,3,2,1,0:T(8,128)(2,1)} %get-tuple-element.122, s32[]{:T(128)} %get-tuple-element.115), kind=kLoop, calls=%fused_computation.16.clone.1 | loop fusion | bytes 16777220 | tf_op jit(solution)/shard_map/while/body/jit(dynamic_index_in_dim)/squeeze | solution.py:66
  223.4 3.2 slice_convert_fusion.2
  226.6 7.2 %fusion.49 = (f32[64,4,32,255]{3,2,1,0:T(8,128)}, f32[64,4,32,255]{3,2,1,0:T(8,128)}) fusion(f32[64,4,32,256]{3,2,1,0:T(8,128)S(1)} %slice_convert_fusion.2), kind=kLoop, calls=%fused_computation.38.clone.1 | loop fusion | bytes 33423360 | tf_op jit(solution)/shard_map/while/body/eval_jaxpr/jit(_roll_static)/slice | solution.py:41
  233.9 6.9 fusion.51
  240.8 7.2 fusion.53
  248.0 6.9 fusion.47
  254.8 3.5 fusion.50
  258.3 4.8 fusion.54
  263.2 1.2 fusion.52
  264.4 1.1 fusion.48
  265.4 36.6 %fusion.55 = f32[2,64,4,32,256]{4,3,2,1,0:T(8,128)} fusion(f32[2,64,4,32,256]{4,3,2,1,0:T(8,128)} %get-tuple-element.116, s32[]{:T(128)} %get-tuple-element.115, f32[64,4,31,256]{3,2,1,0:T(8,128)} %get-tuple-element.94, f32[64,4,1,256]{3,2,1,0:T(1,128)} %get-tuple-element.95, f32[64,4,1,256]{3,2,1,0:T(1,128)S(1)} %get-tuple-element.96, ...), kind=kLoop, calls=%fused_computation.10.clone.1 | loop fusion | flops 65011712 | bytes 110789120 | tf_op jit(solution)/shard_map/while/body/jit(dynamic_update_index_in_dim)/dynamic_update_slice | solution.py:66
  302.3 0.0 copy-start.3
  302.3 18.2 %reshape.27 = f32[128,32768]{1,0:T(8,128)} reshape(f32[2,64,4,32,256]{4,3,2,1,0:T(8,128)} %get-tuple-element.24) | data formatting | bytes 33554432 | tf_op jit(solution)/shard_map/reshape | solution.py:66
  320.5 0.0 copy-done.3
  320.5 13.8 %fusion.14 = bf16[128,32768]{1,0:T(8,128)(2,1)} fusion(f32[128,32768]{1,0:T(8,128)} %reshape.27, bf16[128,32768]{1,0:T(8,128)(2,1)} %bitcast.49, f32[128,128]{1,0:T(8,128)} %all-reduce.4.cloned.1.call-done, f32[128]{0:T(128)S(1)} %copy-done.3), kind=kOutput, calls=%fused_computation.19 | convolution fusion | flops 1082163200 | bytes 33620480 | tf_op jit(solution)/shard_map/dot_general | solution.py:72
  334.3 2.3 collective-permute-start.3
  336.7 0.0 collective-permute-done
  336.7 8.1 %convolution_bitcast_fusion.1 = f32[1,128,128]{2,1,0:T(8,128)S(1)} fusion(bf16[128,32768]{1,0:T(8,128)(2,1)} %bitcast.46, bf16[128,32768]{1,0:T(8,128)(2,1)} %collective-permute-done), kind=kOutput, calls=%fused_computation.26 | convolution fusion | flops 1073741824 | bytes 16842752 | tf_op jit(solution)/shard_map/dot_general | solution.py:48
  344.8 0.0 copy-start.2
  344.8 0.0 copy-start.4
  344.8 83.2 %collective-permute-done.3 = bf16[128,32768]{1,0:T(8,128)(2,1)S(1)} collective-permute-done((bf16[128,32768]{1,0:T(8,128)(2,1)}, bf16[128,32768]{1,0:T(8,128)(2,1)S(1)}, u32[]{:S(2)}, u32[]{:S(2)}) %collective-permute-start.3) | collective-permute-done | bytes 8388640 | tf_op jit(solution)/shard_map/ppermute | solution.py:33
  428.0 5.7 convolution_bitcast_fusion
  433.7 0.7 pad_maximum_fusion.1
  434.4 0.0 all-reduce.6.cloned.1.call-update
  434.4 0.0 copy-done.2
  434.4 0.1 copy.14
  434.5 0.1 broadcast_in_dim.17
  434.6 0.1 reshape.29
  434.7 0.1 constant_dynamic-slice_fusion
  434.8 0.1 copy.15
  434.8 0.0 copy-done.4
  434.8 0.6 dynamic-slice
  436.1 277.8 %all-reduce.6.cloned.1.call-done = f32[2,128,128]{2,1,0:T(8,128)} async-done(((f32[2,128,128]{2,1,0:T(8,128)}), f32[2,128,128]{2,1,0:T(8,128)}) %all-reduce.6.cloned.1.call-update) | async-done | bytes 131088
  713.9 0.7 dynamic-slice_multiply_fusion
  714.6 0.6 slice_bitcast_fusion
  (4 shorter events, 0.0 us)
Async XLA Ops:
  7.2 313.3 %all-reduce.4.cloned.1.call-start = ((), (), s32[]{:S(2)}) async-start(), calls=%async_computation | async-start | bytes 131072 | tf_op jit(solution)/shard_map/psum | solution.py:70
  7.2 14.0 %copy-start = (bf16[128,4,32,256]{3,2,1,0:T(8,128)(2,1)S(1)}, bf16[128,4,32,256]{3,2,1,0:T(8,128)(2,1)}, u32[]{:S(2)}) copy-start(bf16[128,4,32,256]{3,2,1,0:T(8,128)(2,1)} %param.7) | copy-start | bytes 25165828
  14.6 98.7 %collective-permute-start.1 = (bf16[128,2,32,256]{3,2,1,0:T(8,128)(2,1)}, bf16[128,2,32,256]{3,2,1,0:T(8,128)(2,1)}, u32[]{:S(2)}, u32[]{:S(2)}) collective-permute-start(bf16[128,2,32,256]{3,2,1,0:T(8,128)(2,1)} %get-tuple-element.49), channel_id=1, source_target_pairs={{0,1},{1,2},{2,3},{3,4},{4,5},{5,6},{6,7},{7,8},{8,9},{9,10},{10,1... | collective-permute-start | bytes 12582920 | tf_op jit(solution)/shard_map/ppermute | solution.py:21
  16.2 97.2 %collective-permute-start.2 = (bf16[128,2,32,256]{3,2,1,0:T(8,128)(2,1)}, bf16[128,2,32,256]{3,2,1,0:T(8,128)(2,1)}, u32[]{:S(2)}, u32[]{:S(2)}) collective-permute-start(bf16[128,2,32,256]{3,2,1,0:T(8,128)(2,1)} %get-tuple-element.50), channel_id=1, source_target_pairs={{1,0},{2,1},{3,2},{4,3},{5,4},{6,5},{7,6},{8,7},{9,8},{10,9},{11,1... | collective-permute-start | bytes 12582920 | tf_op jit(solution)/shard_map/ppermute | solution.py:23
  42.8 671.1 %all-reduce.6.cloned.1.call-start = ((), (), s32[]{:S(2)}) async-start(), calls=%async_computation.1 | async-start | bytes 262144
  55.4 281.3 %collective-permute-start = (bf16[128,32768]{1,0:T(8,128)(2,1)}, bf16[128,32768]{1,0:T(8,128)(2,1)}, u32[]{:S(2)}, u32[]{:S(2)}) collective-permute-start(bf16[128,32768]{1,0:T(8,128)(2,1)} %bitcast.45), channel_id=1, source_target_pairs={{0,96},{32,0},{64,32},{96,64},{1,97},{33,1},{65,33},{97,65},{2,98}... | collective-permute-start | bytes 25165832 | tf_op jit(solution)/shard_map/ppermute | solution.py:33
  70.8 56.3 %copy-start.1 = (f32[4,32,256]{2,1,0:T(8,128)S(1)}, f32[4,32,256]{2,1,0:T(8,128)}, u32[]{:S(2)}) copy-start(f32[4,32,256]{2,1,0:T(8,128)} %param.8) | copy-start | bytes 393220
  302.3 18.2 %copy-start.3 = (f32[128]{0:T(128)S(1)}, f32[128]{0:T(128)}, u32[]{:S(2)}) copy-start(f32[128]{0:T(128)} %param.10) | copy-start | bytes 1540
  334.3 93.6 %collective-permute-start.3 = (bf16[128,32768]{1,0:T(8,128)(2,1)}, bf16[128,32768]{1,0:T(8,128)(2,1)S(1)}, u32[]{:S(2)}, u32[]{:S(2)}) collective-permute-start(bf16[128,32768]{1,0:T(8,128)(2,1)} %fusion.14), channel_id=1, source_target_pairs={{0,96},{32,0},{64,32},{96,64},{1,97},{33,1},{65,33},{97,65},{2,98}... | collective-permute-start | bytes 25165832 | tf_op jit(solution)/shard_map/ppermute | solution.py:33
  344.8 89.6 %copy-start.2 = (s32[2,2]{1,0:T(2,128)S(1)}, s32[2,2]{1,0:T(2,128)}, u32[]{:S(2)}) copy-start(s32[2,2]{1,0:T(2,128)} %param.11) | copy-start | bytes 52
  344.8 90.0 %copy-start.4 = (u32[128]{0:T(128)S(1)}, u32[128]{0:T(128)}, u32[]{:S(2)}) copy-start(u32[128]{0:T(128)} %constant.35) | copy-start | bytes 1540
Sparse Core Ops, SparseCore 0:
  42.9 272.4 all-reduce.3
  434.5 279.3 all-reduce.5
where the time goes:
time: 733 us; the launch traced here: 722 us
  waiting for transfers between devices  404 us (55%)
  local copies, waits for them, and re-layouts  146 us (20%)
  other arithmetic  95.1 us (13%)
  matrix products  49.2 us (7%)
  between operations  15 us (2%)
  starting transfers between devices  12.3 us (2%)
    unnamed x3, waiting for transfers between devices  278 us
    ppermute x2, waiting for transfers between devices, shifted(): return lax.ppermute(value, axis, pairs)  83.2 us
    dynamic_update_slice x2, other arithmetic, on_device(): lax.map(lambda blk: local_apply(blk, potential), blocks)  73.5 us
    ppermute x1, waiting for transfers between devices, extended(): lax.ppermute(tail, axis, [(i, (i + 1) % count) for i in range(count)])  42.5 us
    slice x8, local copies, waits for them, and re-layouts, local_apply(): far = far + jnp.roll(center, 2, axis) + jnp.roll(center, -2, axis)  40.4 us
    slice x8, local copies, waits for them, and re-layouts, local_apply(): near = near + jnp.roll(center, 1, axis) + jnp.roll(center, -1, axis)  37.4 us
    dot_general x3, matrix products, contract_cells(): lax.dot_general(left, right, (((1,), (1,)), ((), ())), preferred_element_...  35.4 us
    unnamed x13, local copies, waits for them, and re-layouts  25.4 us
  transfers between devices with their start and end apart: 6, of which 3 were waited for; matrix products, arithmetic and copies ran while one was open for 38% of the time, Pallas kernels for 0%

commit v1 on v0

v1 whole, which is shorter than its diff:
```python
import functools

import jax
import jax.numpy as jnp
from jax import lax
from jax.experimental import pallas as pl
from jax.experimental.pallas import tpu as pltpu
from jax.sharding import PartitionSpec as P

W_CENTER = 90.0
W_NEAR = -16.0
W_FAR = 1.0
W_SCALE = 1.0 / 24.0

MESH = pl.DeviceIdType.MESH
CHUNK = 16
PLANES = 4
PARTS = 8


def dot_rows(left, right):
    return lax.dot_general(left, right, (((1,), (1,)), ((), ())), preferred_element_type=jnp.float32)


def kernel(
    orb_hbm, proj_hbm, pot, coupling, pattern, corr_out, ham_out,
    nat, pnat, pt, ext, img, other, circ, coef, acc,
    rc, s1c, qc, s2c, tc, nb, rr, s1, qq, s2,
    in_sem, pin_sem, halo_s, halo_r, pair_s, pair_r, cross_s, cross_r,
    c1_s, c1_r, c2_s, c2_r, n_s, n_r, f1_s, f1_r, f2_s, f2_r,
):
    band = lax.axis_index("band")
    dom = lax.axis_index("dom")
    core = lax.rem(band, 2)
    zh = band // 2
    yz = dom // 4
    xx = lax.rem(dom, 4)
    partner = zh * 2 + (1 - core)
    cross = (1 - zh) * 2 + (1 - core)
    is_even = core == 0
    is_odd = core == 1

    def x_peer(j):
        return yz * 4 + lax.rem(xx + j, 4)

    def yz_peer(j):
        return lax.rem(yz + j, 8) * 4 + xx

    def remote(src, dst, ssem, rsem, to_band, to_dom):
        return pltpu.make_async_remote_copy(
            src_ref=src, dst_ref=dst, send_sem=ssem, recv_sem=rsem,
            device_id=(to_band, to_dom), device_id_type=MESH,
        )

    def plane_of(k):
        return lax.rem(k, 2) * 2 + k // 4

    def rows_of(k):
        return pl.ds(pl.multiple_of(lax.rem(k // 2, 2) * CHUNK, CHUNK), CHUNK)

    def load(src, dst, sem, k):
        return pltpu.make_async_copy(src.at[:, plane_of(k), rows_of(k), :], dst.at[lax.rem(k, 2)], sem.at[lax.rem(k, 2)])

    def own(k):
        return ext.at[plane_of(k) + 2, rows_of(k)]

    def halo(k):
        side = lax.rem(k, 2)
        to_dom = lax.rem(dom + 31 + 2 * side, 32)
        return remote(own(k), ext.at[plane_of(k) + 6 - 8 * side, rows_of(k)], halo_s.at[k], halo_r.at[k], band, to_dom)

    def to_pair(k):
        return remote(own(k), other.at[plane_of(k), rows_of(k), pl.ds(0, 128)], pair_s.at[k], pair_r.at[k], partner, dom)

    def to_cross(k):
        return remote(own(k), other.at[plane_of(k), rows_of(k), pl.ds(128, 128)], cross_s.at[k], cross_r.at[k], cross, dom)

    load(orb_hbm, nat, in_sem, 0).start()
    load(proj_hbm, pnat, pin_sem, 0).start()

    barrier = pltpu.get_barrier_semaphore()
    peers = [(band, x_peer(j)) for j in (1, 2, 3)]
    peers += [(band, yz_peer(j)) for j in range(1, 8)]
    peers += [(cross, yz_peer(j)) for j in range(8)]
    peers += [(partner, dom), (band, lax.rem(dom + 1, 32)), (band, lax.rem(dom + 31, 32))]
    for peer in peers:
        pl.semaphore_signal(barrier, inc=1, device_id=peer, device_id_type=MESH)

    row = lax.broadcasted_iota(jnp.int32, (256, 256), 0)
    col = lax.broadcasted_iota(jnp.int32, (256, 256), 1)
    gap = (row - col) & 255
    near_z = (gap == 1) | (gap == 255)
    far_z = (gap == 2) | (gap == 254)
    circ[...] = jnp.where(gap == 0, W_CENTER, jnp.where(near_z, W_NEAR, jnp.where(far_z, W_FAR, 0.0))).astype(jnp.bfloat16)
    coef[...] = jnp.zeros_like(coef)
    rc[...] = jnp.zeros_like(rc)

    pl.semaphore_wait(barrier, len(peers))

    @pl.loop(0, PARTS)
    def _(k):
        slot = lax.rem(k, 2)

        @pl.when(k + 1 < PARTS)
        def _():
            load(orb_hbm, nat, in_sem, k + 1).start()
            load(proj_hbm, pnat, pin_sem, k + 1).start()

        load(orb_hbm, nat, in_sem, k).wait()
        px = plane_of(k) + 2
        rows = rows_of(k)

        @pl.loop(0, 8)
        def _(q):
            r = pl.ds(pl.multiple_of(q * 16, 16), 16)
            ext[px, rows, r, :] = jnp.swapaxes(nat[slot, r], 0, 1)

        @pl.when(is_even)
        def _():
            halo(k).start()

        @pl.when(is_odd)
        def _():
            to_cross(k).start()
            to_pair(k).start()

        load(proj_hbm, pnat, pin_sem, k).wait()

        @pl.loop(0, 8)
        def _(q):
            r = pl.ds(pl.multiple_of(q * 16, 16), 16)
            pt[:, r, :] = jnp.swapaxes(pnat[slot, r], 0, 1)

        first = lax.rem(k // 2, 2) * CHUNK
        part = coef[...]
        for r in range(CHUNK):
            part = part + dot_rows(pt[r], ext[px, first + r])
        coef[...] = part

    for d in range(32):
        rc[d % 4, d // 4, 0:4, :] = coef[4 * d:4 * d + 4, :]

    def c1(j):
        return remote(rc.at[lax.rem(xx + j, 4)], s1c.at[j], c1_s.at[j], c1_r.at[j], band, x_peer(j))

    def c2(j):
        return remote(qc.at[lax.rem(yz + j, 8)], s2c.at[j], c2_s.at[j], c2_r.at[j], band, yz_peer(j))

    def n_pair():
        return remote(tc, nb.at[0], n_s.at[0], n_r.at[0], partner, dom)

    def n_cross():
        return remote(tc, nb.at[1], n_s.at[1], n_r.at[1], cross, dom)

    for j in (1, 2, 3):
        c1(j).start()

    def local_rows(start, stop):
        def body(k, carry):
            x = k // 32
            y = lax.rem(k, 32)

            def at(dx, dy):
                return ext[x + 2 + dx, lax.rem(y + 32 + dy, 32)].astype(jnp.float32)

            center = ext[x + 2, y]
            own_z = jnp.dot(center, circ[...], preferred_element_type=jnp.float32)
            near = (at(-1, 0) + at(1, 0)) + (at(0, -1) + at(0, 1))
            far = (at(-2, 0) + at(2, 0)) + (at(0, -2) + at(0, 2))
            kinetic = (own_z + W_NEAR * near + far) * W_SCALE
            img[x, y] = (kinetic + pot[x, pl.ds(y, 1), :] * center.astype(jnp.float32)).astype(jnp.bfloat16)
            return carry

        lax.fori_loop(start, stop, body, 0)

    @pl.when(is_even)
    def _():
        for k in (1, 3, 5, 7):
            halo(k).wait_recv()
        local_rows(0, 64)

    def sum_c1():
        for j in (1, 2, 3):
            c1(j).wait_recv()
        qc[...] = (rc[xx] + s1c[1]) + (s1c[2] + s1c[3])
        for j in range(1, 8):
            c2(j).start()

    def sum_c2():
        for j in range(1, 8):
            c2(j).wait_recv()
        total = qc[yz]
        for j in range(1, 8):
            total = total + s2c[j]
        tc[...] = total

    @pl.when(is_odd)
    def _():
        sum_c1()
        sum_c2()
        n_pair().start()
        n_cross().start()

    def weighted(tile):
        r = lax.broadcasted_iota(jnp.int32, (8, 128), 0)
        scale = jnp.zeros((8, 128), jnp.float32)
        for q in range(4):
            scale = jnp.where(r == q, coupling[4 * dom + q], scale)
        return (scale * tile).astype(jnp.bfloat16).astype(jnp.float32)

    def outer(left, right):
        return lax.dot_general(
            left, right, (((0,), (0,)), ((), ())),
            precision=lax.Precision.HIGHEST, preferred_element_type=jnp.float32,
        )

    def f1(j):
        return remote(rr.at[lax.rem(xx + j, 4)], s1.at[j], f1_s.at[j], f1_r.at[j], band, x_peer(j))

    def f2_own(j):
        return remote(qq.at[0, lax.rem(yz + j, 8)], s2.at[j], f2_s.at[j], f2_r.at[j], band, yz_peer(j))

    def f2_cross(j):
        return remote(qq.at[1, lax.rem(yz + j, 8)], s2.at[j], f2_s.at[8 + j], f2_r.at[j], cross, yz_peer(j))

    @pl.when(is_even)
    def _():
        for k in (0, 2, 4, 6):
            halo(k).wait_recv()
        local_rows(64, 128)
        sum_c1()
        acc[...] = jnp.zeros_like(acc)

        @pl.loop(0, PARTS)
        def _(k):
            to_pair(k).wait_recv()
            to_cross(k).wait_recv()
            x = plane_of(k)
            first = lax.rem(k // 2, 2) * CHUNK

            @pl.loop(0, CHUNK // 4)
            def _(q):
                part = acc[...]
                for r in range(4):
                    y = first + q * 4 + r
                    left = jnp.concatenate([ext[x + 2, y], img[x, y]], axis=0)
                    part = part + dot_rows(left, other[x, y])
                acc[...] = part

        sum_c2()
        n_pair().wait_recv()
        n_cross().wait_recv()
        mine = tc[...]
        acc[128:256, 0:128] += outer(mine, weighted(nb[0]))
        acc[128:256, 128:256] += outer(weighted(mine), nb[1])
        acc[0:128, 128:256] = acc[0:128, 128:256].T
        acc[128:256, 128:256] = acc[128:256, 128:256].T
        for d in range(32):
            for half in range(2):
                cols = slice(128 * half, 128 * half + 128)
                rr[d % 4, half, d // 4, 0:4, :] = acc[4 * d:4 * d + 4, cols]
                rr[d % 4, half, d // 4, 4:8, :] = acc[128 + 4 * d:128 + 4 * d + 4, cols]
        for j in (1, 2, 3):
            f1(j).start()
        for j in (1, 2, 3):
            f1(j).wait_recv()
        qq[...] = (rr[xx] + s1[1]) + (s1[2] + s1[3])
        for j in range(8):
            f2_cross(j).start()
        for j in range(1, 8):
            f2_own(j).start()
        for j in range(1, 8):
            f2_own(j).wait_recv()
        s2[0] = qq[0, yz]

    @pl.when(is_odd)
    def _():
        for j in range(8):
            f2_cross(j).wait_recv()

    total = s2[0]
    for j in range(1, 8):
        total = total + s2[j]
    lane = lax.broadcasted_iota(jnp.int32, (8, 128), 1)
    block = dom // 16
    mask = jnp.where(lane < 64, pattern[block, 0], pattern[block, 1]).astype(jnp.float32)
    total = total * mask
    corr_out[...] = total[0:4]
    ham_out[...] = total[4:8]

    for j in (1, 2, 3):
        c1(j).wait_send()
    for j in range(1, 8):
        c2(j).wait_send()

    @pl.when(is_even)
    def _():
        for k in range(PARTS):
            halo(k).wait_send()
        for j in (1, 2, 3):
            f1(j).wait_send()
        for j in range(8):
            f2_cross(j).wait_send()
        for j in range(1, 8):
            f2_own(j).wait_send()

    @pl.when(is_odd)
    def _():
        for k in range(PARTS):
            to_pair(k).wait_send()
            to_cross(k).wait_send()
        n_pair().wait_send()
        n_cross().wait_send()


def on_device(orbitals, potential, projectors, coupling, pattern):
    f32, bf16 = jnp.float32, jnp.bfloat16
    dma = lambda n: pltpu.SemaphoreType.DMA((n,))
    hbm = pl.BlockSpec(memory_space=pl.ANY)
    vmem = pl.BlockSpec(memory_space=pltpu.VMEM)
    smem = pl.BlockSpec(memory_space=pltpu.SMEM)
    return tuple(pl.pallas_call(
        kernel,
        out_shape=[jax.ShapeDtypeStruct((4, 128), f32)] * 2,
        in_specs=[hbm, hbm, vmem, smem, smem],
        out_specs=[vmem, vmem],
        scratch_shapes=[
            pltpu.VMEM((2, 128, CHUNK, 256), bf16),
            pltpu.VMEM((2, 128, CHUNK, 256), bf16),
            pltpu.VMEM((CHUNK, 128, 256), bf16),
            pltpu.VMEM((PLANES + 4, 32, 128, 256), bf16),
            pltpu.VMEM((PLANES, 32, 128, 256), bf16),
            pltpu.VMEM((PLANES, 32, 256, 256), bf16),
            pltpu.VMEM((256, 256), bf16),
            pltpu.VMEM((128, 128), f32),
            pltpu.VMEM((256, 256), f32),
            pltpu.VMEM((4, 8, 8, 128), f32),
            pltpu.VMEM((4, 8, 8, 128), f32),
            pltpu.VMEM((8, 8, 128), f32),
            pltpu.VMEM((8, 8, 128), f32),
            pltpu.VMEM((8, 128), f32),
            pltpu.VMEM((2, 8, 128), f32),
            pltpu.VMEM((4, 2, 8, 8, 128), f32),
            pltpu.VMEM((4, 2, 8, 8, 128), f32),
            pltpu.VMEM((2, 8, 8, 128), f32),
            pltpu.VMEM((8, 8, 128), f32),
            dma(2), dma(2), dma(8), dma(8), dma(8), dma(8), dma(8), dma(8),
            dma(4), dma(4), dma(8), dma(8), dma(2), dma(2), dma(4), dma(4), dma(16), dma(8),
        ],
        compiler_params=pltpu.CompilerParams(
            collective_id=0, has_side_effects=True, vmem_limit_bytes=58 * 2**20,
        ),
    )(orbitals, projectors, potential, coupling, pattern))


def solution(mesh):
    return jax.shard_map(
        on_device,
        mesh=mesh,
        in_specs=(
            P("band", "dom", None, None),
            P("dom", None, None),
            P(None, "dom", None, None),
            P(),
            P("band", None),
        ),
        out_specs=(P(("band", "dom"), None), P(("band", "dom"), None)),
        check_vma=False,
    )
```

time: 733 us -> 163 us (0.22)
  the two profiles are of different devices: /device:TPU:0 before, /device:TPU:1 now
where the time goes in v1:
time: 163 us
  Pallas kernels  160 us (98%)
  local copies, waits for them, and re-layouts  2.48 us (2%)
    pallas_call x1, Pallas kernels, on_device(): pl.pallas_call(kernel, out_shape=[jax.ShapeDtypeStruct((4, 128), f32)] *...  160 us

profile of v1, /device:TPU:1, one launch (start us, length us, event | category | flops | bytes accessed | tf_op | source)
XLA Modules:
  0.0 163.1 jit_solution(3784977226557886893)
XLA Ops:
  0.6 160.0 %shard_map.68 = (f32[4,128]{1,0:T(4,128)}, f32[4,128]{1,0:T(4,128)}) custom-call(bf16[128,4,32,256]{3,2,1,0:T(8,128)(2,1)} %orb_hbm.1, bf16[128,4,32,256]{3,2,1,0:T(8,128)(2,1)} %proj_hbm.1, f32[4,32,256]{2,1,0:T(8,128)} %pot.1, f32[128]{0:T(128)} %coupling.1, s32[2,2]{1,0:T(2,128)} %pattern.1), custom_call_target="tpu_custom_call" | custom-call | tf_op jit(solution)/shard_map/pallas_call | solution.py:322
  160.7 1.2 copy.9
  161.9 1.2 copy.10

commit v2 on v1

--- a/solution.py
+++ b/solution.py
@@ -13,6 +13,8 @@
 W_SCALE = 1.0 / 24.0
 
 MESH = pl.DeviceIdType.MESH
+
+HANDED_ON = {0: ((4, False),), 1: ((0, False), (1, True)), 2: ((2, True), (3, False)), 3: ((7, False),)}
 CHUNK = 16
 PLANES = 4
 PARTS = 8
@@ -24,19 +26,23 @@
 
 def kernel(
     orb_hbm, proj_hbm, pot, coupling, pattern, corr_out, ham_out,
-    nat, pnat, pt, ext, img, other, circ, coef, acc,
+    nat, pnat, pt, ext, far_in, img, other, circ, coef, acc, acc_twin, twin_in,
     rc, s1c, qc, s2c, tc, nb, rr, s1, qq, s2,
     in_sem, pin_sem, halo_s, halo_r, pair_s, pair_r, cross_s, cross_r,
-    c1_s, c1_r, c2_s, c2_r, n_s, n_r, f1_s, f1_r, f2_s, f2_r,
+    c1_s, c1_r, c2_s, c2_r, n_s, n_r, f1_s, f1_r, f2_s, f2_r, via_r, via_s, t_s, t_r,
 ):
     band = lax.axis_index("band")
     dom = lax.axis_index("dom")
     core = lax.rem(band, 2)
     zh = band // 2
     yz = dom // 4
+    zl = lax.rem(yz, 2)
     xx = lax.rem(dom, 4)
     partner = zh * 2 + (1 - core)
     cross = (1 - zh) * 2 + (1 - core)
+    twin = (1 - zh) * 2 + core
+    other_yz = yz + 1 - 2 * lax.rem(yz, 2)
+    row_end = (lax.rem(other_yz * 4 + 31, 32), lax.rem(other_yz * 4 + 4, 32))
     is_even = core == 0
     is_odd = core == 1
 
@@ -55,11 +61,22 @@
     def plane_of(k):
         return lax.rem(k, 2) * 2 + k // 4
 
+    def first_row(k):
+        return (1 - lax.rem(k // 2, 2)) * CHUNK
+
     def rows_of(k):
-        return pl.ds(pl.multiple_of(lax.rem(k // 2, 2) * CHUNK, CHUNK), CHUNK)
-
-    def load(src, dst, sem, k):
-        return pltpu.make_async_copy(src.at[:, plane_of(k), rows_of(k), :], dst.at[lax.rem(k, 2)], sem.at[lax.rem(k, 2)])
+        return pl.ds(pl.multiple_of(first_row(k), CHUNK), CHUNK)
+
+    def pair_order(i):
+        i = lax.rem(i + 4 * (1 - zl), PARTS)
+        return lax.rem(3 * (i // 2), 4) + 4 * lax.rem(i, 2)
+
+    def own_order(i):
+        return i + core * (pair_order(i) - i)
+
+    def load(src, dst, sem, i):
+        k, slot = own_order(i), lax.rem(i, 2)
+        return pltpu.make_async_copy(src.at[:, plane_of(k), rows_of(k), :], dst.at[slot], sem.at[slot])
 
     def own(k):
         return ext.at[plane_of(k) + 2, rows_of(k)]
@@ -69,6 +86,31 @@
         to_dom = lax.rem(dom + 31 + 2 * side, 32)
         return remote(own(k), ext.at[plane_of(k) + 6 - 8 * side, rows_of(k)], halo_s.at[k], halo_r.at[k], band, to_dom)
 
+    def other_odd(flag, z):
+        far = int(flag) + z - 2 * int(flag) * z
+        return partner + far * (cross - partner)
+
+    def to_via(k, flag, column):
+        dst = ext.at[6 - 6 * (k % 2), pl.ds(0, CHUNK)]
+        return remote(own(k), dst, halo_s.at[k], via_r.at[k % 2], other_odd(flag, zl), other_yz * 4 + column)
+
+    def to_twin(k):
+        to_dom = lax.rem(dom + 31 + 2 * lax.rem(k, 2), 32)
+        return remote(own(k), far_in.at[k // 4], halo_s.at[k], halo_r.at[k], twin, to_dom)
+
+    def via_in(k):
+        dst = ext.at[6 - 6 * (k % 2), pl.ds(0, CHUNK)]
+        return remote(dst, dst, via_s.at[k % 2], via_r.at[k % 2], partner, row_end[0])
+
+    def via(k, far):
+        side = k % 2
+        src = ext.at[6 - 6 * side, pl.ds(0, CHUNK)]
+        dst = far_in.at[k // 4] if far else ext.at[plane_of(k) + 6 - 8 * side, rows_of(k)]
+        return remote(src, dst, via_s.at[side], halo_r.at[k], partner, row_end[side])
+
+    def twin_sum():
+        return remote(acc_twin, twin_in, t_s.at[0], t_r.at[0], twin, dom)
+
     def to_pair(k):
         return remote(own(k), other.at[plane_of(k), rows_of(k), pl.ds(0, 128)], pair_s.at[k], pair_r.at[k], partner, dom)
 
@@ -82,9 +124,37 @@
     peers = [(band, x_peer(j)) for j in (1, 2, 3)]
     peers += [(band, yz_peer(j)) for j in range(1, 8)]
     peers += [(cross, yz_peer(j)) for j in range(8)]
-    peers += [(partner, dom), (band, lax.rem(dom + 1, 32)), (band, lax.rem(dom + 31, 32))]
+    peers += [(partner, dom), (twin, dom)]
+    peers += [(b, lax.rem(dom + step, 32)) for b in (band, twin) for step in (1, 31)]
     for peer in peers:
         pl.semaphore_signal(barrier, inc=1, device_id=peer, device_id_type=MESH)
+
+    def greet(peer):
+        pl.semaphore_signal(barrier, inc=1, device_id=peer, device_id_type=MESH)
+
+    up_end = is_even & (xx == 3)
+    down_end = is_even & (xx == 0)
+    ahead = lax.rem(yz + 1, 8)
+    back = lax.rem(yz + 7, 8)
+
+    for column, chunks in HANDED_ON.items():
+
+        @pl.when(is_odd & (xx == column))
+        def _():
+            for k, flag in chunks:
+                greet((other_odd(flag, 1 - zl), other_yz * 4 + 3 * (k % 2)))
+                greet((partner, row_end[k % 2]))
+
+    for end, side, last in ((up_end, 1, ahead), (down_end, 0, back)):
+
+        @pl.when(end)
+        def _():
+            for column, chunks in HANDED_ON.items():
+                for k, flag in chunks:
+                    if k % 2 == side:
+                        greet((other_odd(flag, zl), other_yz * 4 + column))
+                    else:
+                        greet((partner, (last + 1 - 2 * lax.rem(last, 2)) * 4 + column))
 
     row = lax.broadcasted_iota(jnp.int32, (256, 256), 0)
     col = lax.broadcasted_iota(jnp.int32, (256, 256), 1)
@@ -95,18 +165,39 @@
     coef[...] = jnp.zeros_like(coef)
     rc[...] = jnp.zeros_like(rc)
 
-    pl.semaphore_wait(barrier, len(peers))
+    at_end = up_end | down_end
+    edge = (xx == 0) | (xx == 3)
+    kinds = (
+        (at_end, 6),
+        (is_odd & edge, 2),
+        (is_odd & jnp.logical_not(edge), 4),
+        (is_even & jnp.logical_not(edge), 0),
+    )
+    for kind, count in kinds:
+
+        @pl.when(kind)
+        def _():
+            pl.semaphore_wait(barrier, len(peers) + count)
+
+    @pl.when(down_end)
+    def _():
+        ext[0:2, pl.ds(pl.multiple_of(CHUNK * zl, CHUNK), CHUNK), :, :] = jnp.zeros((2, CHUNK, 128, 256), jnp.bfloat16)
+
+    @pl.when(up_end)
+    def _():
+        ext[6:8, pl.ds(pl.multiple_of(CHUNK * (1 - zl), CHUNK), CHUNK), :, :] = jnp.zeros((2, CHUNK, 128, 256), jnp.bfloat16)
 
     @pl.loop(0, PARTS)
-    def _(k):
-        slot = lax.rem(k, 2)
-
-        @pl.when(k + 1 < PARTS)
-        def _():
-            load(orb_hbm, nat, in_sem, k + 1).start()
-            load(proj_hbm, pnat, pin_sem, k + 1).start()
-
-        load(orb_hbm, nat, in_sem, k).wait()
+    def _(i):
+        slot = lax.rem(i, 2)
+        k = own_order(i)
+
+        @pl.when(i + 1 < PARTS)
+        def _():
+            load(orb_hbm, nat, in_sem, i + 1).start()
+            load(proj_hbm, pnat, pin_sem, i + 1).start()
+
+        load(orb_hbm, nat, in_sem, i).wait()
         px = plane_of(k) + 2
         rows = rows_of(k)
 
@@ -117,21 +208,37 @@
 
         @pl.when(is_even)
         def _():
-            halo(k).start()
+            for column, chunks in HANDED_ON.items():
+                for c, flag in chunks:
+
+                    @pl.when((up_end if c % 2 else down_end) & (k == c))
+                    def _():
+                        to_via(c, flag, column).start()
+
+            straight = (down_end & (k == 6)) | (up_end & (k == 5))
+            across = (down_end & (slot == 0)) | (up_end & (slot == 1))
+
+            @pl.when(straight & (zl == 0))
+            def _():
+                to_twin(k).start()
+
+            @pl.when(jnp.logical_not(across) | (straight & (zl == 1)))
+            def _():
+                halo(k).start()
 
         @pl.when(is_odd)
         def _():
             to_cross(k).start()
             to_pair(k).start()
 
-        load(proj_hbm, pnat, pin_sem, k).wait()
+        load(proj_hbm, pnat, pin_sem, i).wait()
 
         @pl.loop(0, 8)
         def _(q):
             r = pl.ds(pl.multiple_of(q * 16, 16), 16)
             pt[:, r, :] = jnp.swapaxes(pnat[slot, r], 0, 1)
 
-        first = lax.rem(k // 2, 2) * CHUNK
+        first = first_row(k)
         part = coef[...]
         for r in range(CHUNK):
             part = part + dot_rows(pt[r], ext[px, first + r])
@@ -173,11 +280,23 @@
 
         lax.fori_loop(start, stop, body, 0)
 
-    @pl.when(is_even)
-    def _():
+    def first_planes():
         for k in (1, 3, 5, 7):
             halo(k).wait_recv()
         local_rows(0, 64)
+
+    def last_planes():
+        for k in (0, 2, 4, 6):
+            halo(k).wait_recv()
+        local_rows(64, 128)
+
+    @pl.when(down_end)
+    def _():
+        last_planes()
+
+    @pl.when(is_even & (xx != 0))
+    def _():
+        first_planes()
 
     def sum_c1():
         for j in (1, 2, 3):
@@ -194,6 +313,16 @@
             total = total + s2c[j]
         tc[...] = total
 
+    for column, chunks in HANDED_ON.items():
+
+        for z in range(2):
+
+            @pl.when(is_odd & (xx == column) & (zl == z))
+            def _():
+                for k, flag in chunks:
+                    via_in(k).wait_recv()
+                    via(k, flag == (z == 1)).start()
+
     @pl.when(is_odd)
     def _():
         sum_c1()
@@ -223,20 +352,25 @@
     def f2_cross(j):
         return remote(qq.at[1, lax.rem(yz + j, 8)], s2.at[j], f2_s.at[8 + j], f2_r.at[j], cross, yz_peer(j))
 
+    @pl.when(down_end)
+    def _():
+        first_planes()
+
+    @pl.when(is_even & (xx != 0))
+    def _():
+        last_planes()
+
     @pl.when(is_even)
     def _():
-        for k in (0, 2, 4, 6):
-            halo(k).wait_recv()
-        local_rows(64, 128)
         sum_c1()
         acc[...] = jnp.zeros_like(acc)
 
-        @pl.loop(0, PARTS)
-        def _(k):
+        def products(i):
+            k = pair_order(i)
             to_pair(k).wait_recv()
             to_cross(k).wait_recv()
             x = plane_of(k)
-            first = lax.rem(k // 2, 2) * CHUNK
+            first = first_row(k)
 
             @pl.loop(0, CHUNK // 4)
             def _(q):
@@ -246,6 +380,39 @@
                     left = jnp.concatenate([ext[x + 2, y], img[x, y]], axis=0)
                     part = part + dot_rows(left, other[x, y])
                 acc[...] = part
+
+        pl.loop(0, 4)(products)
+
+        def twin_products(first, outer_plane, inner_plane, near_at, far_at):
+            acc_twin[...] = jnp.zeros_like(acc_twin)
+
+            @pl.loop(0, CHUNK)
+            def _(r):
+                near = far_in[near_at, r].astype(jnp.float32)
+                far = far_in[far_at, r].astype(jnp.float32)
+                outer_part = ((W_NEAR * near + W_FAR * far) * W_SCALE).astype(jnp.bfloat16)
+                inner_part = ((W_FAR * W_SCALE) * near).astype(jnp.bfloat16)
+                acc_twin[...] += dot_rows(outer_part, other[outer_plane, first + r]) + dot_rows(
+                    inner_part, other[inner_plane, first + r]
+                )
+
+            twin_sum().start()
+
+        @pl.when(down_end)
+        def _():
+            twin_products(CHUNK * zl, 0, 1, 1, 0)
+
+        @pl.when(up_end)
+        def _():
+            twin_products(CHUNK * (1 - zl), 3, 2, 0, 1)
+
+        pl.loop(4, PARTS)(products)
+
+        @pl.when(at_end)
+        def _():
+            twin_sum().wait_recv()
+            acc[128:256, 0:128] += twin_in[:, 128:256]
+            acc[128:256, 128:256] += twin_in[:, 0:128]
 
         sum_c2()
         n_pair().wait_recv()
@@ -312,6 +479,17 @@
         n_pair().wait_send()
         n_cross().wait_send()
 
+    for column, chunks in HANDED_ON.items():
+
+        @pl.when(is_odd & (xx == column))
+        def _():
+            for k, _flag in chunks:
+                via(k, False).wait_send()
+
+    @pl.when(at_end)
+    def _():
+        twin_sum().wait_send()
+
 
 def on_device(orbitals, potential, projectors, coupling, pattern):
     f32, bf16 = jnp.float32, jnp.bfloat16
@@ -329,11 +507,14 @@
             pltpu.VMEM((2, 128, CHUNK, 256), bf16),
             pltpu.VMEM((CHUNK, 128, 256), bf16),
             pltpu.VMEM((PLANES + 4, 32, 128, 256), bf16),
+            pltpu.VMEM((2, CHUNK, 128, 256), bf16),
             pltpu.VMEM((PLANES, 32, 128, 256), bf16),
             pltpu.VMEM((PLANES, 32, 256, 256), bf16),
             pltpu.VMEM((256, 256), bf16),
             pltpu.VMEM((128, 128), f32),
             pltpu.VMEM((256, 256), f32),
+            pltpu.VMEM((128, 256), f32),
+            pltpu.VMEM((128, 256), f32),
             pltpu.VMEM((4, 8, 8, 128), f32),
             pltpu.VMEM((4, 8, 8, 128), f32),
             pltpu.VMEM((8, 8, 128), f32),
@@ -345,7 +526,7 @@
             pltpu.VMEM((2, 8, 8, 128), f32),
             pltpu.VMEM((8, 8, 128), f32),
             dma(2), dma(2), dma(8), dma(8), dma(8), dma(8), dma(8), dma(8),
-            dma(4), dma(4), dma(8), dma(8), dma(2), dma(2), dma(4), dma(4), dma(16), dma(8),
+            dma(4), dma(4), dma(8), dma(8), dma(2), dma(2), dma(4), dma(4), dma(16), dma(8), dma(2), dma(2), dma(1), dma(1),
         ],
         compiler_params=pltpu.CompilerParams(
             collective_id=0, has_side_effects=True, vmem_limit_bytes=58 * 2**20,

time: 163 us -> 134 us (0.82)
  Pallas kernels: 160 us -> 130 us
    pallas_call x1, Pallas kernels: 160 us -> 130 us  [on_device(): pl.pallas_call(kernel, out_shape=[jax.ShapeDtypeStruct((4, 128), f32)] *...]
where the time goes in v2:
time: 134 us; the launch traced here: 133 us
  Pallas kernels  130 us (97%)
  local copies, waits for them, and re-layouts  2.48 us (2%)
    pallas_call x1, Pallas kernels, on_device(): pl.pallas_call(kernel, out_shape=[jax.ShapeDtypeStruct((4, 128), f32)] *...  130 us

profile of v2, /device:TPU:1, one launch (start us, length us, event | category | flops | bytes accessed | tf_op | source)
XLA Modules:
  0.0 133.4 jit_solution(14257382763045263327)
XLA Ops:
  0.6 130.3 %shard_map.68 = (f32[4,128]{1,0:T(4,128)}, f32[4,128]{1,0:T(4,128)}) custom-call(bf16[128,4,32,256]{3,2,1,0:T(8,128)(2,1)} %orb_hbm.1, bf16[128,4,32,256]{3,2,1,0:T(8,128)(2,1)} %proj_hbm.1, f32[4,32,256]{2,1,0:T(8,128)} %pot.1, f32[128]{0:T(128)} %coupling.1, s32[2,2]{1,0:T(2,128)} %pattern.1), custom_call_target="tpu_custom_call" | custom-call | tf_op jit(solution)/shard_map/pallas_call | solution.py:500
  130.9 1.2 copy.9
  132.2 1.2 copy.10
